TPU v7x, 32 devices: a whole 2x2x4 slice. The times are simulated.
32 devices in a mesh: dp: 4 (over x, core), prec: 4 (over z), pair: 2 (over y).
Axes of the slice: x: 2, y: 2, z: 4, core: 2. Of those that a mesh axis runs over, the one named last changes fastest.
Arguments:
- activations: bfloat16 [1024, 4096], P('dp', 'prec')
- output_grads: bfloat16 [1024, 16384], P('dp', 'pair')
- iter_counts: int32 [32, 8], P(('pair', 'dp'), 'prec'), may hold values from 1 to 2, as said below
Outputs:
- preconditioned: float32 [16384, 4096], P(('pair', 'dp'), 'prec')
Inputs may be any that keep to these rules, and one draw needn't show every extreme that they name: `iter_counts`: newton iterations of each block; 2 is taken by at least one block in every draw.
All inputs are finite; a program needn't handle non-finite values.
Results may differ from a plain program's by a relative error of at most 0.0003.
Values may be sent and summed in bfloat16 or wider, within the bound.
A program may use at most 128 MiB of HBM per device.

v0:
```python
import jax
import jax.numpy as jnp
from jax import lax
from jax.sharding import PartitionSpec as P

BLK = 512


SHIFT = 0.001


def product(left, right):
    return jnp.dot(left, right, precision=lax.Precision.HIGHEST)


def inverse_root(statistic, plan):
    extent = statistic.shape[0]
    identity = jnp.eye(extent, dtype=statistic.dtype)
    shifted = statistic + SHIFT * identity
    scaling = 2.5 / jnp.sqrt(jnp.sum(shifted * shifted) + 1e-06)
    inverse = identity * jnp.sqrt(jnp.sqrt(scaling))
    coupled = shifted * scaling

    def advance(step_index, state_pair):
        current, matrix = state_pair
        factor = 1.25 * identity - 0.25 * matrix
        square = product(factor, factor)
        return (product(current, factor), product(product(square, square), matrix))

    inverse, coupled = lax.fori_loop(0, plan, advance, (inverse, coupled))
    return inverse


def both_roots(item):
    block, plan = item
    left_root = inverse_root(product(block, block.T), plan)
    right_root = inverse_root(product(block.T, block), plan)
    return (left_root, right_root)


def per_device(activations, output_grads, iter_counts):
    dp_size = lax.axis_size("dp")
    row_count = output_grads.shape[1] // dp_size
    feature_count = activations.shape[1]
    contract = (((0,), (0,)), ((), ()))
    grad_block = lax.psum_scatter(
        lax.dot_general(output_grads, activations, contract, preferred_element_type=jnp.float32),
        "dp",
        scatter_dimension=0,
        tiled=True,
    )
    ff_blocks = row_count // BLK
    d_blocks = feature_count // BLK
    blocks = (
        grad_block.reshape(ff_blocks, BLK, d_blocks, BLK)
        .transpose(0, 2, 1, 3)
        .reshape(ff_blocks * d_blocks, BLK, BLK)
    )
    plan = iter_counts.reshape(-1)
    left_roots, right_roots = lax.map(both_roots, (blocks, plan))
    highest = lax.Precision.HIGHEST
    updates = jnp.einsum(
        "bij,bjk->bik",
        jnp.einsum("bij,bjk->bik", left_roots, blocks, precision=highest),
        right_roots,
        precision=highest,
    )
    grad_squares, update_squares = lax.psum(
        (jnp.sum(blocks * blocks), jnp.sum(updates * updates)), ("dp", "prec", "pair")
    )
    graft_ratio = jnp.sqrt(grad_squares / update_squares)
    scaled = updates * graft_ratio
    return (
        scaled.reshape(ff_blocks, d_blocks, BLK, BLK)
        .transpose(0, 2, 1, 3)
        .reshape(row_count, feature_count)
    )


def solution(mesh):
    in_specs = (P("dp", "prec"), P("dp", "pair"), P(("pair", "dp"), "prec"))
    out_specs = P(("pair", "dp"), "prec")
    return jax.shard_map(
        per_device, mesh=mesh, in_specs=in_specs, out_specs=out_specs, check_vma=False
    )
```

profile of v0, /device:TPU:0, one launch (start us, length us, event | category | flops | bytes accessed | tf_op | source)
XLA Modules:
  0.0 702.5 jit_solution(4307757550110552437)
XLA Ops:
  7.6 15.4 %fusion.42 = f32[8192,1024]{1,0:T(8,128)} fusion(bf16[256,8192]{1,0:T(8,128)(2,1)} %param.10, bf16[256,1024]{1,0:T(8,128)(2,1)S(1)} %copy-done), kind=kOutput, calls=%fused_computation.58 | convolution fusion | flops 4294967296 | bytes 38273024 | tf_op jit(solution)/shard_map/dot_general | solution.py:47
  23.8 237.0 %reduce-scatter.2.cloned.1.call-done = f32[2048,1024]{1,0:T(8,128)} async-done(((f32[8192,1024]{1,0:T(8,128)}), f32[2048,1024]{1,0:T(8,128)}) %reduce-scatter.2.cloned.1.call-update) | async-done | bytes 8388624 | tf_op jit(solution)/shard_map/reduce_scatter | solution.py:46
  260.8 11.7 %reshape.15 = f32[4,512,2,512]{3,2,1,0:T(2,128)} reshape(f32[2048,1024]{1,0:T(8,128)} %reduce-scatter.2.cloned.1.call-done) | data formatting | bytes 16777216 | tf_op jit(solution)/shard_map/reshape | solution.py:55
  272.6 12.6 %multiply_reduce_fusion.3 = f32[]{:T(128)} fusion(f32[4,512,2,512]{3,2,1,0:T(2,128)} %reshape.15), kind=kLoop, calls=%fused_computation.52 | loop fusion | flops 4194303 | bytes 8388612 | tf_op jit(solution)/shard_map/reduce_sum | solution.py:69
  285.2 8.1 %copy.12 = f32[4,2,512,512]{3,2,1,0:T(8,128)} copy(f32[4,2,512,512]{3,1,2,0:T(2,128)} %bitcast.75) | data formatting | bytes 16777216 | tf_op jit(solution)/shard_map/transpose | solution.py:56
  293.3 290.2 %while.40 = (s32[]{:T(128)}, f32[8,512,512]{1,2,0:T(8,128)}, f32[8,512,512]{1,2,0:T(8,128)}, f32[8,512,512]{2,1,0:T(8,128)}, s32[8]{0:T(128)S(1)}, /*index=5*/s3...) while((s32[]{:T(128)}, f32[8,512,512]{1,2,0:T(8,128)}, ...), condition=%wide.region_8.9_spmd, body=%wide.region_1.8_spmd.sunk | while | flops 16114515968 | bytes 48236488 | solution.py:60
  299.6 9.0 %while.42 = (s32[]{:T(128)}, f32[512,512]{0,1:T(8,128)S(1)}, f32[512,512]{1,0:T(8,128)S(1)}, s32[]{:T(128)}, s32[]{:T(128)}) while((s32[]{:T(128)}, f32[512,512]{0,1:T(8,128)S(1)}, f32[512,512]{1,0:T(8,128)S(1)}, s32[]{:T(128)}, s32[]{:T(128)}) %tuple.73), condition=%wide.region_4.4_spmd.clone, body=%wide.region_3.3_spmd.clone.sunk | while | flops 6444548096 | bytes 14680125 | solution.py:30
  316.2 9.0 %while.41 = (s32[]{:T(128)}, f32[512,512]{0,1:T(8,128)S(1)}, f32[512,512]{1,0:T(8,128)S(1)}, s32[]{:T(128)}, s32[]{:T(128)}) while((s32[]{:T(128)}, f32[512,512]{0,1:T(8,128)S(1)}, f32[512,512]{1,0:T(8,128)S(1)}, s32[]{:T(128)}, s32[]{:T(128)}) %tuple.70), condition=%wide.region_7.7_spmd.clone, body=%wide.region_6.6_spmd.clone.sunk | while | flops 6444548096 | bytes 14680125 | solution.py:30
  326.7 4.2 multiply_reduce_fusion.7
  332.8 9.0 %while.42 = (s32[]{:T(128)}, f32[512,512]{0,1:T(8,128)S(1)}, f32[512,512]{1,0:T(8,128)S(1)}, s32[]{:T(128)}, s32[]{:T(128)}) while((s32[]{:T(128)}, f32[512,512]{0,1:T(8,128)S(1)}, f32[512,512]{1,0:T(8,128)S(1)}, s32[]{:T(128)}, s32[]{:T(128)}) %tuple.73), condition=%wide.region_4.4_spmd.clone, body=%wide.region_3.3_spmd.clone.sunk | while | flops 6444548096 | bytes 14680125 | solution.py:30
  341.8 4.2 multiply_reduce_fusion.6
  349.5 9.0 %while.41 = (s32[]{:T(128)}, f32[512,512]{0,1:T(8,128)S(1)}, f32[512,512]{1,0:T(8,128)S(1)}, s32[]{:T(128)}, s32[]{:T(128)}) while((s32[]{:T(128)}, f32[512,512]{0,1:T(8,128)S(1)}, f32[512,512]{1,0:T(8,128)S(1)}, s32[]{:T(128)}, s32[]{:T(128)}) %tuple.70), condition=%wide.region_7.7_spmd.clone, body=%wide.region_6.6_spmd.clone.sunk | while | flops 6444548096 | bytes 14680125 | solution.py:30
  366.0 9.0 %while.42 = (s32[]{:T(128)}, f32[512,512]{0,1:T(8,128)S(1)}, f32[512,512]{1,0:T(8,128)S(1)}, s32[]{:T(128)}, s32[]{:T(128)}) while((s32[]{:T(128)}, f32[512,512]{0,1:T(8,128)S(1)}, f32[512,512]{1,0:T(8,128)S(1)}, s32[]{:T(128)}, s32[]{:T(128)}) %tuple.73), condition=%wide.region_4.4_spmd.clone, body=%wide.region_3.3_spmd.clone.sunk | while | flops 6444548096 | bytes 14680125 | solution.py:30
  382.7 9.0 %while.41 = (s32[]{:T(128)}, f32[512,512]{0,1:T(8,128)S(1)}, f32[512,512]{1,0:T(8,128)S(1)}, s32[]{:T(128)}, s32[]{:T(128)}) while((s32[]{:T(128)}, f32[512,512]{0,1:T(8,128)S(1)}, f32[512,512]{1,0:T(8,128)S(1)}, s32[]{:T(128)}, s32[]{:T(128)}) %tuple.70), condition=%wide.region_7.7_spmd.clone, body=%wide.region_6.6_spmd.clone.sunk | while | flops 6444548096 | bytes 14680125 | solution.py:30
  399.1 9.0 %while.42 = (s32[]{:T(128)}, f32[512,512]{0,1:T(8,128)S(1)}, f32[512,512]{1,0:T(8,128)S(1)}, s32[]{:T(128)}, s32[]{:T(128)}) while((s32[]{:T(128)}, f32[512,512]{0,1:T(8,128)S(1)}, f32[512,512]{1,0:T(8,128)S(1)}, s32[]{:T(128)}, s32[]{:T(128)}) %tuple.73), condition=%wide.region_4.4_spmd.clone, body=%wide.region_3.3_spmd.clone.sunk | while | flops 6444548096 | bytes 14680125 | solution.py:30
  415.7 9.0 %while.41 = (s32[]{:T(128)}, f32[512,512]{0,1:T(8,128)S(1)}, f32[512,512]{1,0:T(8,128)S(1)}, s32[]{:T(128)}, s32[]{:T(128)}) while((s32[]{:T(128)}, f32[512,512]{0,1:T(8,128)S(1)}, f32[512,512]{1,0:T(8,128)S(1)}, s32[]{:T(128)}, s32[]{:T(128)}) %tuple.70), condition=%wide.region_7.7_spmd.clone, body=%wide.region_6.6_spmd.clone.sunk | while | flops 6444548096 | bytes 14680125 | solution.py:30
  432.2 9.0 %while.42 = (s32[]{:T(128)}, f32[512,512]{0,1:T(8,128)S(1)}, f32[512,512]{1,0:T(8,128)S(1)}, s32[]{:T(128)}, s32[]{:T(128)}) while((s32[]{:T(128)}, f32[512,512]{0,1:T(8,128)S(1)}, f32[512,512]{1,0:T(8,128)S(1)}, s32[]{:T(128)}, s32[]{:T(128)}) %tuple.73), condition=%wide.region_4.4_spmd.clone, body=%wide.region_3.3_spmd.clone.sunk | while | flops 6444548096 | bytes 14680125 | solution.py:30
  448.8 9.0 %while.41 = (s32[]{:T(128)}, f32[512,512]{0,1:T(8,128)S(1)}, f32[512,512]{1,0:T(8,128)S(1)}, s32[]{:T(128)}, s32[]{:T(128)}) while((s32[]{:T(128)}, f32[512,512]{0,1:T(8,128)S(1)}, f32[512,512]{1,0:T(8,128)S(1)}, s32[]{:T(128)}, s32[]{:T(128)}) %tuple.70), condition=%wide.region_7.7_spmd.clone, body=%wide.region_6.6_spmd.clone.sunk | while | flops 6444548096 | bytes 14680125 | solution.py:30
  465.3 17.3 %while.42 = (s32[]{:T(128)}, f32[512,512]{0,1:T(8,128)S(1)}, f32[512,512]{1,0:T(8,128)S(1)}, s32[]{:T(128)}, s32[]{:T(128)}) while((s32[]{:T(128)}, f32[512,512]{0,1:T(8,128)S(1)}, f32[512,512]{1,0:T(8,128)S(1)}, s32[]{:T(128)}, s32[]{:T(128)}) %tuple.73), condition=%wide.region_4.4_spmd.clone, body=%wide.region_3.3_spmd.clone.sunk | while | flops 6444548096 | bytes 14680125 | solution.py:30
  490.3 17.3 %while.41 = (s32[]{:T(128)}, f32[512,512]{0,1:T(8,128)S(1)}, f32[512,512]{1,0:T(8,128)S(1)}, s32[]{:T(128)}, s32[]{:T(128)}) while((s32[]{:T(128)}, f32[512,512]{0,1:T(8,128)S(1)}, f32[512,512]{1,0:T(8,128)S(1)}, s32[]{:T(128)}, s32[]{:T(128)}) %tuple.70), condition=%wide.region_7.7_spmd.clone, body=%wide.region_6.6_spmd.clone.sunk | while | flops 6444548096 | bytes 14680125 | solution.py:30
  509.1 4.3 multiply_reduce_fusion.7
  515.3 9.0 %while.42 = (s32[]{:T(128)}, f32[512,512]{0,1:T(8,128)S(1)}, f32[512,512]{1,0:T(8,128)S(1)}, s32[]{:T(128)}, s32[]{:T(128)}) while((s32[]{:T(128)}, f32[512,512]{0,1:T(8,128)S(1)}, f32[512,512]{1,0:T(8,128)S(1)}, s32[]{:T(128)}, s32[]{:T(128)}) %tuple.73), condition=%wide.region_4.4_spmd.clone, body=%wide.region_3.3_spmd.clone.sunk | while | flops 6444548096 | bytes 14680125 | solution.py:30
  524.3 4.3 multiply_reduce_fusion.6
  532.1 9.0 %while.41 = (s32[]{:T(128)}, f32[512,512]{0,1:T(8,128)S(1)}, f32[512,512]{1,0:T(8,128)S(1)}, s32[]{:T(128)}, s32[]{:T(128)}) while((s32[]{:T(128)}, f32[512,512]{0,1:T(8,128)S(1)}, f32[512,512]{1,0:T(8,128)S(1)}, s32[]{:T(128)}, s32[]{:T(128)}) %tuple.70), condition=%wide.region_7.7_spmd.clone, body=%wide.region_6.6_spmd.clone.sunk | while | flops 6444548096 | bytes 14680125 | solution.py:30
  548.5 9.0 %while.42 = (s32[]{:T(128)}, f32[512,512]{0,1:T(8,128)S(1)}, f32[512,512]{1,0:T(8,128)S(1)}, s32[]{:T(128)}, s32[]{:T(128)}) while((s32[]{:T(128)}, f32[512,512]{0,1:T(8,128)S(1)}, f32[512,512]{1,0:T(8,128)S(1)}, s32[]{:T(128)}, s32[]{:T(128)}) %tuple.73), condition=%wide.region_4.4_spmd.clone, body=%wide.region_3.3_spmd.clone.sunk | while | flops 6444548096 | bytes 14680125 | solution.py:30
  565.2 9.0 %while.41 = (s32[]{:T(128)}, f32[512,512]{0,1:T(8,128)S(1)}, f32[512,512]{1,0:T(8,128)S(1)}, s32[]{:T(128)}, s32[]{:T(128)}) while((s32[]{:T(128)}, f32[512,512]{0,1:T(8,128)S(1)}, f32[512,512]{1,0:T(8,128)S(1)}, s32[]{:T(128)}, s32[]{:T(128)}) %tuple.70), condition=%wide.region_7.7_spmd.clone, body=%wide.region_6.6_spmd.clone.sunk | while | flops 6444548096 | bytes 14680125 | solution.py:30
  583.5 16.5 %fusion.43 = f32[8,512,512]{2,1,0:T(8,128)S(1)} fusion(f32[8,512,512]{1,2,0:T(8,128)} %get-tuple-element.89, f32[8,512,512]{2,1,0:T(8,128)} %get-tuple-element.347), kind=kOutput, calls=%fused_computation.59 | convolution fusion | flops 12884901888 | bytes 25165824 | tf_op jit(solution)/shard_map/bij,bjk->bik/dot_general | solution.py:64
  600.1 16.9 %multiply_reduce_fusion.2 = (f32[]{:T(128)}, f32[8,512,512]{2,1,0:T(8,128)}) fusion(f32[8,512,512]{2,1,0:T(8,128)S(1)} %fusion.43, f32[8,512,512]{1,2,0:T(8,128)S(1)} %copy-done.2), kind=kOutput, calls=%fused_computation.51 | convolution fusion | flops 12889096192 | bytes 25165828 | tf_op jit(solution)/shard_map/bij,bjk->bik/dot_general | solution.py:62
  617.0 54.9 %all-reduce = (f32[]{:T(128)}, f32[]{:T(128)}) all-reduce(f32[]{:T(128)} %multiply_reduce_fusion.3, f32[]{:T(128)} %get-tuple-element.163), channel_id=1, replica_groups=mesh['dp'=4,'prec'=4,'pair'=2] {'dp','prec','pair'}, use_global_device_ids=true, to_apply=%region_10.11 | all-reduce | flops 2 | bytes 16 | tf_op jit(solution)/shard_map/psum | solution.py:68
  673.1 4.4 broadcast_multiply_fusion.2
  677.5 12.4 %copy.15 = f32[4,512,2,512]{3,2,1,0:T(2,128)S(1)} copy(f32[4,512,2,512]{3,1,2,0:T(8,128)S(1)} %bitcast.77) | data formatting | bytes 16777216 | tf_op jit(solution)/shard_map/transpose | solution.py:75
  689.9 5.5 copy.17
  (198 shorter events, 232.9 us)
Async XLA Ops:
  6.5 1.0 copy-start
  6.5 254.3 %reduce-scatter.2.cloned.1.call-start = ((), (), s32[]{:S(2)}) async-start(), calls=%async_computation.1 | async-start | bytes 41943040 | tf_op jit(solution)/shard_map/reduce_scatter | solution.py:46
  22.9 0.7 copy-start.3
  583.5 16.5 %copy-start.2 = (f32[8,512,512]{1,2,0:T(8,128)S(1)}, f32[8,512,512]{1,2,0:T(8,128)}, u32[]{:S(2)}) copy-start(f32[8,512,512]{1,2,0:T(8,128)} %get-tuple-element.90) | copy-start | bytes 25165828
  689.9 5.5 copy-start.1
Sparse Core Ops, SparseCore 0:
  23.1 237.6 reduce-scatter.1
where the time goes:
time: 713 us; the launch traced here: 702 us
  matrix products  250 us (35%)
  waiting for transfers between devices  237 us (33%)
  local copies, waits for them, and re-layouts  74.3 us (10%)
  blocking collectives  54.9 us (8%)
  loops' own time  42.2 us (6%)
  other arithmetic  28.9 us (4%)
  between operations  14.9 us (2%)
    reduce_scatter x1, waiting for transfers between devices, per_device(): lax.psum_scatter(lax.dot_general(output_grads, activations, contract, pre...  237 us
    dot_general x88, matrix products, product(): return jnp.dot(left, right, precision=lax.Precision.HIGHEST)  201 us
    psum x1, blocking collectives, per_device(): lax.psum((jnp.sum(blocks * blocks), jnp.sum(updates * updates)), ('dp', '...  54.9 us
    another operation x16, loops' own time, inverse_root(): inverse, coupled = lax.fori_loop(0, plan, advance, (inverse, coupled))  22.4 us
    another operation x1, loops' own time, per_device(): left_roots, right_roots = lax.map(both_roots, (blocks, plan))  19.8 us
    while x52, local copies, waits for them, and re-layouts  17.6 us
    dot_general x1, matrix products, per_device(): jnp.einsum('bij,bjk->bik', jnp.einsum('bij,bjk->bik', left_roots, blocks,...  16.9 us
    dot_general x1, matrix products, per_device(): jnp.einsum('bij,bjk->bik', left_roots, blocks, precision=highest)  16.5 us
  transfers between devices with their start and end apart: 1, of which 1 were waited for; matrix products, arithmetic and copies ran while one was open for 0% of the time, Pallas kernels for 0%

commit v1 on v0

v1 whole, which is shorter than its diff:
```python
import functools
import jax
import jax.numpy as jnp
from jax import lax
from jax.experimental import pallas as pl
from jax.experimental.pallas import tpu as pltpu
from jax.sharding import PartitionSpec as P

BLK = 512
SHIFT = 0.001
NN = (((1,), (0,)), ((), ()))
NT = (((1,), (1,)), ((), ()))
TN = (((0,), (0,)), ((), ()))


def halves(x):
    high = x.astype(jnp.bfloat16)
    low = (x - high.astype(jnp.float32)).astype(jnp.bfloat16)
    return high, low


def dot(a, b, dims):
    return lax.dot_general(a, b, dims, preferred_element_type=jnp.float32)


def product(a, b, dims=NN):
    return dot(a[0], b[0], dims) + (dot(a[0], b[1], dims) + dot(a[1], b[0], dims))


def total(x):
    return jnp.sum(x, keepdims=True)


def first_iteration(g):
    gs = halves(g)
    left = product(gs, gs, NT)
    trace = total(g * g)
    norm = total(left * left) + (2.0 * SHIFT) * trace + BLK * SHIFT * SHIFT
    scaling = 2.5 / jnp.sqrt(norm + 1e-06)
    a = 1.25 - (0.25 * SHIFT) * scaling
    b = 0.25 * scaling
    ls = halves(left)
    half = a * g - b * product(ls, gs)
    update = (a * half - b * product(ls, halves(half))) * jnp.sqrt(scaling)
    return left, scaling, trace, update


def identity():
    rows = lax.broadcasted_iota(jnp.int32, (BLK, BLK), 0)
    return (rows == lax.broadcasted_iota(jnp.int32, (BLK, BLK), 1)).astype(jnp.float32)


def later_iterations(count, coupled_ref, update_ref):
    def advance(_, carry):
        coupled = coupled_ref[...]
        factor = halves(1.25 * identity() - 0.25 * coupled)
        square = halves(product(factor, factor))
        fourth = halves(product(square, square))
        coupled = product(fourth, halves(coupled))
        coupled_ref[...] = coupled
        factor = halves(1.25 * identity() - 0.25 * coupled)
        once = product(factor, halves(update_ref[...]))
        update_ref[...] = product(factor, halves(once))
        return carry

    lax.fori_loop(1, count, advance, 0)


def block_kernel(counts_ref, og_ref, act_ref, update_ref, squares_ref, coupled_ref):
    i, j = pl.program_id(0), pl.program_id(1)

    @pl.when((i == 0) & (j == 0))
    def _():
        squares_ref[...] = jnp.zeros_like(squares_ref)

    g = dot(og_ref[...], act_ref[...], TN)
    left, scaling, trace, update = first_iteration(g)
    update_ref[...] = update
    count = counts_ref[i, j]

    @pl.when(count > 1)
    def _():
        coupled_ref[...] = scaling * (left + SHIFT * identity())
        later_iterations(count, coupled_ref, update_ref)

    u = update_ref[...]
    squares_ref[0:8, :] += jnp.broadcast_to(trace, (8, 128))
    squares_ref[8:16, :] += jnp.broadcast_to(total(u * u), (8, 128))


def local_updates(og, act, counts):
    tokens, rows = og.shape
    features = act.shape[1]
    grid = (rows // BLK, features // BLK)
    return pl.pallas_call(
        block_kernel,
        grid=grid,
        in_specs=[
            pl.BlockSpec(memory_space=pltpu.SMEM),
            pl.BlockSpec((tokens, BLK), lambda i, j: (0, i)),
            pl.BlockSpec((tokens, BLK), lambda i, j: (0, j)),
        ],
        out_specs=[
            pl.BlockSpec((BLK, BLK), lambda i, j: (i, j)),
            pl.BlockSpec((16, 128), lambda i, j: (0, 0)),
        ],
        out_shape=[
            jax.ShapeDtypeStruct((rows, features), jnp.float32),
            jax.ShapeDtypeStruct((16, 128), jnp.float32),
        ],
        scratch_shapes=[pltpu.VMEM((BLK, BLK), jnp.float32)],
        compiler_params=pltpu.CompilerParams(vmem_limit_bytes=48 * 2**20),
    )(counts, og, act)


def per_device(activations, output_grads, iter_counts):
    act = lax.all_gather(activations, "dp", axis=0, tiled=True)
    og = lax.all_to_all(output_grads, "dp", split_axis=1, concat_axis=0, tiled=True)
    updates, squares = local_updates(og, act, iter_counts)
    sums = lax.psum(squares, ("dp", "prec", "pair"))
    return updates * jnp.sqrt(sums[0, 0] / sums[8, 0])


def solution(mesh):
    in_specs = (P("dp", "prec"), P("dp", "pair"), P(("pair", "dp"), "prec"))
    out_specs = P(("pair", "dp"), "prec")
    return jax.shard_map(
        per_device, mesh=mesh, in_specs=in_specs, out_specs=out_specs, check_vma=False
    )
```

time: 713 us -> 180 us (0.25); the launches traced: 702 us -> 178 us
  matrix products: 250 us -> 0 us
  waiting for transfers between devices: 237 us -> 60.7 us
  local copies, waits for them, and re-layouts: 74.3 us -> 7.08 us
  loops' own time: 42.2 us -> 0 us
  Pallas kernels: 0 us -> 32.8 us
  other arithmetic: 28.9 us -> 8.69 us
    dot_general x91 -> x0, matrix products: 250 us -> none  [the longest x88 201 us: product(): return jnp.dot(left, right, precision=lax.Precision.HIGHEST)]
    reduce_scatter x1 -> x0, waiting for transfers between devices: 237 us -> none  [per_device(): lax.psum_scatter(lax.dot_general(output_grads, activations, contract, pre...]
    another operation x17 -> x0, loops' own time: 42.2 us -> none  [the longest x16 22.4 us: inverse_root(): inverse, coupled = lax.fori_loop(0, plan, advance, (inverse, coupled))]
    pallas_call x0 -> x1, Pallas kernels: none -> 32.8 us  [local_updates(): pl.pallas_call(block_kernel, grid=grid, in_specs=[pl.BlockSpec(memory_spa...]
    all_to_all x0 -> x1, waiting for transfers between devices: none -> 31.6 us  [per_device(): lax.all_to_all(output_grads, 'dp', split_axis=1, concat_axis=0, tiled=True)]
    all_gather x0 -> x1, waiting for transfers between devices: none -> 28.4 us  [per_device(): act = lax.all_gather(activations, 'dp', axis=0, tiled=True)]
    transpose x2 -> x0, local copies, waits for them, and re-layouts: 20.5 us -> none  [the longest x1 12.4 us: per_device(): return scaled.reshape(ff_blocks, d_blocks, BLK, BLK).transpose(0, 2, 1, 3...]
    while x52 -> x0, local copies, waits for them, and re-layouts: 17.6 us -> none
  transfers between devices with their start and end apart: 1 -> 2, of which waited for: 1 -> 2; matrix products, arithmetic and copies ran while one was open for 0% -> 3% of each run, Pallas kernels for 0% -> 0%
where the time goes in v1:
time: 180 us; the launch traced here: 178 us
  waiting for transfers between devices  60.7 us (34%)
  blocking collectives  49.1 us (27%)
  Pallas kernels  32.8 us (18%)
  between operations  14.8 us (8%)
  other arithmetic  8.69 us (5%)
  local copies, waits for them, and re-layouts  7.08 us (4%)
  starting transfers between devices  4.84 us (3%)
    psum x1, blocking collectives, per_device(): sums = lax.psum(squares, ('dp', 'prec', 'pair'))  49.1 us
    pallas_call x1, Pallas kernels, local_updates(): pl.pallas_call(block_kernel, grid=grid, in_specs=[pl.BlockSpec(memory_spa...  32.8 us
    all_to_all x1, waiting for transfers between devices, per_device(): lax.all_to_all(output_grads, 'dp', split_axis=1, concat_axis=0, tiled=True)  31.6 us
    all_gather x1, waiting for transfers between devices, per_device(): act = lax.all_gather(activations, 'dp', axis=0, tiled=True)  28.4 us
    mul x1, other arithmetic, per_device(): return updates * jnp.sqrt(sums[0, 0] / sums[8, 0])  8.69 us
    all_to_all x1, starting transfers between devices, per_device(): lax.all_to_all(output_grads, 'dp', split_axis=1, concat_axis=0, tiled=True)  4.84 us
    all_to_all x1, local copies, waits for them, and re-layouts, per_device(): lax.all_to_all(output_grads, 'dp', split_axis=1, concat_axis=0, tiled=True)  4.79 us
  transfers between devices with their start and end apart: 2, of which 2 were waited for; matrix products, arithmetic and copies ran while one was open for 3% of the time, Pallas kernels for 0%

profile of v1, /device:TPU:0, one launch (start us, length us, event | category | flops | bytes accessed | tf_op | source)
XLA Modules:
  0.0 178.0 jit_solution(13503354217688938122)
XLA Ops:
  6.5 0.0 all-gather.2.cloned.1.call-start
  6.5 0.7 all-gather.2.cloned.1.call-update
  7.3 0.0 copy-start.1
  7.3 4.8 %copy.8 = bf16[32,4,8,2048]{3,2,0,1:T(8,128)(2,1)} copy(bf16[32,4,8,2048]{3,2,1,0:T(8,128)(2,1)} %bitcast.9) | data formatting | bytes 8388608 | tf_op jit(solution)/shard_map/all_to_all | solution.py:118
  12.1 4.8 %all-to-all-start = ((bf16[256,4,2048]{2,0,1:T(8,128)(2,1)}), bf16[256,4,2048]{2,0,1:T(8,128)(2,1)}, u32[]{:S(2)}, u32[]{:S(2)}) async-start(bf16[256,4,2048]{2,0,1:T(8,128)(2,1)} %bitcast.8), calls=%async_computation | async-start | bytes 8388608 | tf_op jit(solution)/shard_map/all_to_all | solution.py:118
  16.9 0.0 copy-done.1
  16.9 0.1 copy.5.counts_ref
  17.0 28.4 %all-gather.2.cloned.1.call-done.act_ref = bf16[1024,1024]{1,0:T(8,128)(2,1)} async-done(((bf16[256,1024]{1,0:T(8,128)(2,1)}), bf16[1024,1024]{1,0:T(8,128)(2,1)}) %all-gather.2.cloned.1.call-update) | async-done | bytes 2097168 | tf_op jit(solution)/shard_map/all_gather | solution.py:117
  45.4 31.6 %all-to-all-done = bf16[256,4,2048]{2,0,1:T(8,128)(2,1)} async-done(((bf16[256,4,2048]{2,0,1:T(8,128)(2,1)}), bf16[256,4,2048]{2,0,1:T(8,128)(2,1)}, u32[]{:S(2)}, u32[]{:S(2)}) %all-to-all-start) | async-done | bytes 4194336 | tf_op jit(solution)/shard_map/all_to_all | solution.py:118
  77.0 0.0 copy-start
  77.0 1.6 copy-done
  78.6 32.8 %shard_map.37 = (f32[2048,1024]{1,0:T(8,128)}, f32[16,128]{1,0:T(8,128)S(1)}) custom-call(s32[4,2]{1,0:T(4,128)S(1)} %copy.5.counts_ref, bf16[1024,2048]{1,0:T(8,128)(2,1)} %bitcast.1.og_ref, bf16[1024,1024]{1,0:T(8,128)(2,1)S(1)} %copy-done), custom_call_target="tpu_custom_call" | custom-call | tf_op jit(solution)/shard_map/pallas_call | solution.py:95
  111.4 49.1 %psum.7 = f32[16,128]{1,0:T(8,128)S(1)} all-reduce(f32[16,128]{1,0:T(8,128)S(1)} %get-tuple-element.8), channel_id=1, replica_groups=mesh['dp'=4,'prec'=4,'pair'=2] {'dp','prec','pair'}, use_global_device_ids=true, to_apply=%region_0.0 | all-reduce | flops 2048 | bytes 16384 | tf_op jit(solution)/shard_map/psum | solution.py:120
  160.5 0.6 fusion
  162.5 8.7 %broadcast_multiply_fusion = f32[2048,1024]{1,0:T(8,128)} fusion(f32[2048,1024]{1,0:T(8,128)} %get-tuple-element.7, f32[]{:T(128)} %bitcast.2), kind=kLoop, calls=%fused_computation.1 | loop fusion | flops 2097152 | bytes 16777220 | tf_op jit(solution)/shard_map/mul | solution.py:121
Async XLA Ops:
  6.5 38.9 %all-gather.2.cloned.1.call-start = ((), (), s32[]{:S(2)}) async-start(), calls=%async_computation.1 | async-start | bytes 2621440 | tf_op jit(solution)/shard_map/all_gather | solution.py:117
  7.3 9.7 %copy-start.1 = (s32[4,2]{0,1:T(2,128)S(1)}, s32[4,2]{0,1:T(2,128)}, u32[]{:S(2)}) copy-start(s32[4,2]{0,1:T(2,128)} %param.5) | copy-start | bytes 100
  12.1 64.9 %all-to-all-start = ((bf16[256,4,2048]{2,0,1:T(8,128)(2,1)}), bf16[256,4,2048]{2,0,1:T(8,128)(2,1)}, u32[]{:S(2)}, u32[]{:S(2)}) async-start(bf16[256,4,2048]{2,0,1:T(8,128)(2,1)} %bitcast.8), calls=%async_computation | async-start | bytes 8388608 | tf_op jit(solution)/shard_map/all_to_all | solution.py:118
  77.0 1.6 copy-start
Sparse Core Ops, SparseCore 0:
  8.9 36.4 all-gather.1

commit v2 on v1

--- a/solution.py
+++ b/solution.py
@@ -113,12 +113,371 @@
     )(counts, og, act)
 
 
-def per_device(activations, output_grads, iter_counts):
+def remote(src, dst, send, recv, **device):
+    return pltpu.make_async_remote_copy(
+        src_ref=src, dst_ref=dst, send_sem=send, recv_sem=recv,
+        device_id=device, device_id_type=pl.DeviceIdType.MESH,
+    )
+
+
+def gather_kernel(
+    og_ref, act_ref, update_ref, left_ref, stats_ref,
+    og_all, act_all, update_all, left_all,
+    og_own, og_cs, og_cr, og_xs, og_xr, og_zs, og_zr,
+    act_own, act_cs, act_cr, act_xs, act_xr, act_ys, act_yr, act_fs, act_fr,
+    update_sem, left_sem,
+):
+    shard = og_ref.shape[0]
+    half = shard // 2
+    chunks, features = og_all.shape[0], act_all.shape[0]
+    width = chunks * BLK
+    me, z, y = lax.axis_index("dp"), lax.axis_index("prec"), lax.axis_index("pair")
+    x, core = lax.div(me, 2), lax.rem(me, 2)
+    mate, over, base = me + 1 - 2 * core, me + 2 - 4 * x, 2 - 2 * x
+    over_mate = base + 1 - core
+    side = lax.rem(z, 2)
+    z_mate, y_mate = z + 1 - 2 * side, 1 - y
+
+    def span(start, size):
+        return pl.ds(pl.multiple_of(start, 128), size)
+
+    def og_columns(device, a):
+        return span(device * width + a * BLK, BLK)
+
+    def og_rows(a, device, part):
+        return og_all.at[a, span(device * shard + part * half, half)]
+
+    def act_rows(j, device, part):
+        return act_all.at[j, span(device * shard + part * half, half)]
+
+    def own_og(a):
+        return pltpu.make_async_copy(
+            og_ref.at[:, og_columns(me, a)], og_all.at[a, span(me * shard, shard)], og_own.at[a]
+        )
+
+    def own_act(j):
+        return pltpu.make_async_copy(
+            act_ref.at[:, pl.ds(j * BLK, BLK)], act_all.at[j, span(me * shard, shard)], act_own.at[j]
+        )
+
+    def core_og(a):
+        return remote(
+            og_ref.at[:, og_columns(mate, a)], og_all.at[a, span(me * shard, shard)],
+            og_cs.at[a], og_cr.at[a], dp=mate,
+        )
+
+    def core_act(j):
+        return remote(
+            act_ref.at[:, pl.ds(j * BLK, BLK)], act_all.at[j, span(me * shard, shard)],
+            act_cs.at[j], act_cr.at[j], dp=mate,
+        )
+
+    def x_og(a, k):
+        return remote(
+            og_ref.at[span(side * half, half), og_columns(base + k, a)], og_rows(a, me, side),
+            og_xs.at[a, k], og_xr.at[a, core], dp=base + k,
+        )
+
+    def x_og_arrived(a, k):
+        there = og_rows(a, base + k, side)
+        remote(there, there, og_xs.at[a, k], og_xr.at[a, k], dp=base + k).wait_recv()
+
+    def z_og(a, k):
+        there = og_rows(a, base + k, side)
+        return remote(there, there, og_zs.at[a, k], og_zr.at[a, k], prec=z_mate)
+
+    def x_act(j):
+        return remote(
+            act_ref.at[span(y * half, half), pl.ds(j * BLK, BLK)], act_rows(j, me, y),
+            act_xs.at[j], act_xr.at[j], dp=over,
+        )
+
+    def y_act(j):
+        there = act_rows(j, over, y)
+        return remote(there, there, act_ys.at[j], act_yr.at[j], pair=y_mate)
+
+    def f_act(j, k):
+        there = act_rows(j, over, y if k == 0 else y_mate)
+        return remote(there, there, act_fs.at[j, k], act_fr.at[j, k], dp=mate)
+
+    barrier = pltpu.get_barrier_semaphore()
+    for device in (dict(dp=mate), dict(dp=base), dict(dp=base + 1), dict(prec=z_mate), dict(pair=y_mate)):
+        pl.semaphore_signal(barrier, inc=1, device_id=device, device_id_type=pl.DeviceIdType.MESH)
+    pl.semaphore_wait(barrier, 5)
+
+    def send_x(a):
+        x_og(a, 0).start()
+        x_og(a, 1).start()
+
+    def pass_on_og(a):
+        for k in range(2):
+            x_og_arrived(a, k)
+            z_og(a, k).start()
+
+    def pass_on_act(j):
+        x_act(j).wait_recv()
+        y_act(j).start()
+        f_act(j, 0).start()
+
+    def pass_on_act_again(j):
+        y_act(j).wait_recv()
+        f_act(j, 1).start()
+
+    x_act(0).start()
+    send_x(0)
+    for j in range(1, features):
+        x_act(j).start()
+    if chunks > 1:
+        send_x(1)
+    for j in range(features):
+        core_act(j).start()
+        own_act(j).start()
+    for a in range(chunks):
+        core_og(a).start()
+        own_og(a).start()
+    pass_on_act(0)
+    pass_on_og(0)
+    if chunks > 2:
+        send_x(2)
+    pass_on_act_again(0)
+    for j in range(1, features):
+        pass_on_act(j)
+    for j in range(1, features):
+        pass_on_act_again(j)
+    for j in range(features):
+        own_act(j).wait()
+        core_act(j).wait_recv()
+        f_act(j, 0).wait_recv()
+        f_act(j, 1).wait_recv()
+
+    def outgoing(s):
+        a, j = lax.div(s, features), lax.rem(s, features)
+        place = update_ref.at[span(a * BLK, BLK), span(j * BLK, BLK)]
+        return (
+            pltpu.make_async_copy(update_all.at[s], place, update_sem.at[s]),
+            pltpu.make_async_copy(left_all.at[s], left_ref.at[s], left_sem.at[s]),
+        )
+
+    def step(s, carry):
+        a, j = lax.div(s, features), lax.rem(s, features)
+
+        @pl.when(j == 0)
+        def _():
+            own_og(a).wait()
+            core_og(a).wait_recv()
+            z_og(a, 0).wait_recv()
+            z_og(a, 1).wait_recv()
+
+        g = dot(og_all[a], act_all[j], TN)
+        left, scaling, trace, update = first_iteration(g)
+        update_all[s] = update
+        left_all[s] = left
+        for copy in outgoing(s):
+            copy.start()
+        stats_ref[s, 0:1, :] = jnp.broadcast_to(trace, (1, 128))
+        stats_ref[s, 1:2, :] = jnp.broadcast_to(total(update * update), (1, 128))
+        stats_ref[s, 2:3, :] = jnp.broadcast_to(scaling, (1, 128))
+        stats_ref[s, 3:8, :] = jnp.zeros((5, 128), jnp.float32)
+
+        @pl.when((j == 0) & (a + 1 < chunks))
+        def _():
+            pass_on_og(a + 1)
+
+        @pl.when((j == 0) & (a + 3 < chunks))
+        def _():
+            send_x(a + 3)
+
+        return carry
+
+    lax.fori_loop(0, chunks * features, step, 0)
+
+    for a in range(chunks):
+        core_og(a).wait_send()
+        for k in range(2):
+            x_og(a, k).wait_send()
+            z_og(a, k).wait_send()
+    for j in range(features):
+        core_act(j).wait_send()
+        x_act(j).wait_send()
+        y_act(j).wait_send()
+        f_act(j, 0).wait_send()
+        f_act(j, 1).wait_send()
+    for s in range(chunks * features):
+        for copy in outgoing(s):
+            copy.wait()
+
+
+def gathered_updates(og, act):
+    shard, rows = og.shape[0], og.shape[1] // lax.axis_size("dp")
+    tokens, width = shard * lax.axis_size("dp"), act.shape[1]
+    chunks, features = rows // BLK, width // BLK
+    blocks = chunks * features
+    anywhere = pl.BlockSpec(memory_space=pl.ANY)
+    one = pltpu.SemaphoreType.DMA((chunks,))
+    two = pltpu.SemaphoreType.DMA((chunks, 2))
+    act_one = pltpu.SemaphoreType.DMA((features,))
+    act_two = pltpu.SemaphoreType.DMA((features, 2))
+    return pl.pallas_call(
+        gather_kernel,
+        in_specs=[anywhere, anywhere],
+        out_specs=[anywhere, anywhere, pl.BlockSpec(memory_space=pltpu.VMEM)],
+        out_shape=[
+            jax.ShapeDtypeStruct((rows, width), jnp.float32),
+            jax.ShapeDtypeStruct((blocks, BLK, BLK), jnp.float32),
+            jax.ShapeDtypeStruct((blocks, 8, 128), jnp.float32),
+        ],
+        scratch_shapes=[
+            pltpu.VMEM((chunks, tokens, BLK), jnp.bfloat16),
+            pltpu.VMEM((features, tokens, BLK), jnp.bfloat16),
+            pltpu.VMEM((blocks, BLK, BLK), jnp.float32),
+            pltpu.VMEM((blocks, BLK, BLK), jnp.float32),
+            one, one, one, two, two, two, two,
+            act_one, act_one, act_one, act_one, act_one, act_one, act_one, act_two, act_two,
+            pltpu.SemaphoreType.DMA((blocks,)),
+            pltpu.SemaphoreType.DMA((blocks,)),
+        ],
+        compiler_params=pltpu.CompilerParams(
+            collective_id=0, has_side_effects=True, vmem_limit_bytes=56 * 2**20
+        ),
+    )(og, act)
+
+
+def finish_kernel(counts_ref, stats_ref, left_ref, update_in, update_ref, squares_ref, coupled_ref, block_ref, sem):
+    del update_in
+    features = counts_ref.shape[1]
+    squares_ref[...] = jnp.zeros_like(squares_ref)
+
+    def step(s, carry):
+        a, j = lax.div(s, features), lax.rem(s, features)
+        count = counts_ref[a, j]
+        squares_ref[0:8, :] += jnp.broadcast_to(stats_ref[s, 0:1, :], (8, 128))
+
+        @pl.when(count <= 1)
+        def _():
+            squares_ref[8:16, :] += jnp.broadcast_to(stats_ref[s, 1:2, :], (8, 128))
+
+        @pl.when(count > 1)
+        def _():
+            place = update_ref.at[
+                pl.ds(pl.multiple_of(a * BLK, BLK), BLK), pl.ds(pl.multiple_of(j * BLK, BLK), BLK)
+            ]
+            left_in = pltpu.make_async_copy(left_ref.at[s], coupled_ref, sem.at[0])
+            block_in = pltpu.make_async_copy(place, block_ref, sem.at[1])
+            left_in.start()
+            block_in.start()
+            left_in.wait()
+            block_in.wait()
+            coupled_ref[...] = stats_ref[s, 2:3, 0:1] * (coupled_ref[...] + SHIFT * identity())
+            later_iterations(count, coupled_ref, block_ref)
+            block_out = pltpu.make_async_copy(block_ref, place, sem.at[2])
+            block_out.start()
+            u = block_ref[...]
+            squares_ref[8:16, :] += jnp.broadcast_to(total(u * u), (8, 128))
+            block_out.wait()
+
+        return carry
+
+    lax.fori_loop(0, counts_ref.shape[0] * features, step, 0)
+
+
+def finished_updates(counts, stats, left, updates):
+    anywhere = pl.BlockSpec(memory_space=pl.ANY)
+    vmem = pl.BlockSpec(memory_space=pltpu.VMEM)
+    return pl.pallas_call(
+        finish_kernel,
+        in_specs=[pl.BlockSpec(memory_space=pltpu.SMEM), vmem, anywhere, anywhere],
+        out_specs=[anywhere, vmem],
+        out_shape=[
+            jax.ShapeDtypeStruct(updates.shape, jnp.float32),
+            jax.ShapeDtypeStruct((16, 128), jnp.float32),
+        ],
+        scratch_shapes=[
+            pltpu.VMEM((BLK, BLK), jnp.float32),
+            pltpu.VMEM((BLK, BLK), jnp.float32),
+            pltpu.SemaphoreType.DMA((3,)),
+        ],
+        input_output_aliases={3: 0},
+        compiler_params=pltpu.CompilerParams(vmem_limit_bytes=56 * 2**20),
+    )(counts, stats, left, updates)
+
+
+def ratio_kernel(axes, squares_ref, ratio_ref, *scratch):
+    buffers, sends, recvs = scratch[0:3], scratch[3:6], scratch[6:9]
+    barrier = pltpu.get_barrier_semaphore()
+    partners = 0
+    for name, size in axes:
+        for step in range(1, size):
+            other = lax.rem(lax.axis_index(name) + step, size)
+            pl.semaphore_signal(
+                barrier, inc=1, device_id={name: other}, device_id_type=pl.DeviceIdType.MESH
+            )
+            partners += 1
+    pl.semaphore_wait(barrier, partners)
+    sums = squares_ref[...]
+    for (name, size), buffer, send, recv in zip(axes, buffers, sends, recvs):
+        me = lax.axis_index(name)
+        buffer[me] = sums
+        copies = []
+        for step in range(1, size):
+            copy = remote(
+                buffer.at[me], buffer.at[me], send.at[step - 1], recv.at[step - 1],
+                **{name: lax.rem(me + step, size)},
+            )
+            copy.start()
+            copies.append(copy)
+        for copy in copies:
+            copy.wait()
+        sums = buffer[0]
+        for i in range(1, size):
+            sums = sums + buffer[i]
+    ratio_ref[...] = jnp.sqrt(sums[0:8, :] / sums[8:16, :])
+
+
+def graft_ratio(squares):
+    axes = [(name, lax.axis_size(name)) for name in ("dp", "prec", "pair")]
+    vmem = pl.BlockSpec(memory_space=pltpu.VMEM)
+    sems = [pltpu.SemaphoreType.DMA((max(size - 1, 1),)) for _, size in axes]
+    return pl.pallas_call(
+        functools.partial(ratio_kernel, axes),
+        in_specs=[vmem],
+        out_specs=vmem,
+        out_shape=jax.ShapeDtypeStruct((8, 128), jnp.float32),
+        scratch_shapes=[pltpu.VMEM((size, 16, 128), jnp.float32) for _, size in axes] + sems + sems,
+        compiler_params=pltpu.CompilerParams(collective_id=1, has_side_effects=True),
+    )(squares)
+
+
+def scale_kernel(ratio_ref, update_ref, out_ref):
+    out_ref[...] = update_ref[...] * ratio_ref[0:1, 0:1]
+
+
+def scaled_updates(ratio, updates):
+    rows, width = updates.shape
+    block = pl.BlockSpec((BLK // 2, width), lambda i: (i, 0))
+    return pl.pallas_call(
+        scale_kernel,
+        grid=(rows // (BLK // 2),),
+        in_specs=[pl.BlockSpec(memory_space=pltpu.VMEM), block],
+        out_specs=block,
+        out_shape=jax.ShapeDtypeStruct(updates.shape, jnp.float32),
+        compiler_params=pltpu.CompilerParams(vmem_limit_bytes=48 * 2**20),
+    )(ratio, updates)
+
+
+def gathered_first(activations, output_grads, iter_counts):
     act = lax.all_gather(activations, "dp", axis=0, tiled=True)
     og = lax.all_to_all(output_grads, "dp", split_axis=1, concat_axis=0, tiled=True)
-    updates, squares = local_updates(og, act, iter_counts)
-    sums = lax.psum(squares, ("dp", "prec", "pair"))
-    return updates * jnp.sqrt(sums[0, 0] / sums[8, 0])
+    return local_updates(og, act, iter_counts)
+
+
+def per_device(activations, output_grads, iter_counts):
+    sizes = [lax.axis_size(name) for name in ("dp", "prec", "pair")]
+    if sizes[0] == 4 and sizes[1] % 2 == 0 and sizes[2] == 2:
+        updates, left, stats = gathered_updates(output_grads, activations)
+        updates, squares = finished_updates(iter_counts, stats, left, updates)
+    else:
+        updates, squares = gathered_first(activations, output_grads, iter_counts)
+    return scaled_updates(graft_ratio(squares), updates)
 
 
 def solution(mesh):

time: 180 us -> 102 us (0.57); the launches traced: 178 us -> 102 us
  Pallas kernels: 32.8 us -> 100 us
  waiting for transfers between devices: 60.7 us -> 0 us
  blocking collectives: 49.1 us -> 0 us
  between operations: 14.8 us -> 0.03 us
  other arithmetic: 8.69 us -> 0 us
  local copies, waits for them, and re-layouts: 7.08 us -> 1.99 us
  starting transfers between devices: 4.84 us -> 0 us
    pallas_call x1 -> x4, Pallas kernels: 32.8 us -> 100 us  [the longest x1 64.7 us: gathered_updates(): pl.pallas_call(gather_kernel, in_specs=[anywhere, anywhere], out_specs=[a...]
    psum x1 -> x0, blocking collectives: 49.1 us -> none  [per_device(): sums = lax.psum(squares, ('dp', 'prec', 'pair'))]
    all_to_all x1 -> x0, waiting for transfers between devices: 31.6 us -> none  [per_device(): lax.all_to_all(output_grads, 'dp', split_axis=1, concat_axis=0, tiled=True)]
    all_gather x1 -> x0, waiting for transfers between devices: 28.4 us -> none  [per_device(): act = lax.all_gather(activations, 'dp', axis=0, tiled=True)]
    mul x1 -> x0, other arithmetic: 8.69 us -> none  [per_device(): return updates * jnp.sqrt(sums[0, 0] / sums[8, 0])]
    all_to_all x1 -> x0, starting transfers between devices: 4.84 us -> none  [per_device(): lax.all_to_all(output_grads, 'dp', split_axis=1, concat_axis=0, tiled=True)]
    all_to_all x1 -> x0, local copies, waits for them, and re-layouts: 4.79 us -> none  [per_device(): lax.all_to_all(output_grads, 'dp', split_axis=1, concat_axis=0, tiled=True)]
  transfers between devices with their start and end apart: 2 -> 0, of which waited for: 2 -> 0; matrix products, arithmetic and copies ran while one was open for 3% -> 0% of each run, Pallas kernels for 0% -> 0%
where the time goes in v2:
time: 102 us
  Pallas kernels  100 us (98%)
  local copies, waits for them, and re-layouts  1.99 us (2%)
    pallas_call x1, Pallas kernels, gathered_updates(): pl.pallas_call(gather_kernel, in_specs=[anywhere, anywhere], out_specs=[a...  64.7 us
    pallas_call x1, Pallas kernels, graft_ratio(): pl.pallas_call(functools.partial(ratio_kernel, axes), in_specs=[vmem], ou...  24.9 us
    pallas_call x1, Pallas kernels, scaled_updates(): pl.pallas_call(scale_kernel, grid=(rows // (BLK // 2),), in_specs=[pl.Blo...  9.08 us

profile of v2, /device:TPU:0, one launch (start us, length us, event | category | flops | bytes accessed | tf_op | source)
XLA Modules:
  0.0 102.3 jit_solution(13951041211931580686)
XLA Ops:
  0.0 1.3 %copy.5.counts_ref = s32[4,2]{1,0:T(4,128)} copy(s32[4,2]{0,1:T(2,128)} %param.5) | data formatting | bytes 64 | tf_op args[2]
  1.3 64.7 %shard_map.37 = (f32[2048,1024]{1,0:T(8,128)}, f32[8,512,512]{2,1,0:T(8,128)}, f32[8,8,128]{2,1,0:T(8,128)}) custom-call(bf16[256,8192]{1,0:T(8,128)(2,1)} %og_ref.1, bf16[256,1024]{1,0:T(8,128)(2,1)} %act_ref.1), custom_call_target="tpu_custom_call" | custom-call | tf_op jit(solution)/shard_map/pallas_call | solution.py:320
  66.1 1.6 %shard_map.38 = (f32[2048,1024]{1,0:T(8,128)}, f32[16,128]{1,0:T(8,128)}) custom-call(s32[4,2]{1,0:T(4,128)} %copy.5.counts_ref, f32[8,8,128]{2,1,0:T(8,128)} %get-tuple-element.10.stats_ref, f32[8,512,512]{2,1,0:T(8,128)} %get-tuple-element.11.left_ref, f32[2048,1024]{1,0:T(8,128)} %get-tuple-element.12.update_in), custom_call_target="tpu_custom_call", output_to_operand_aliasing={{0}: (3, {})} | custom-call | tf_op jit(solution)/shard_map/pallas_call | solution.py:386
  67.6 24.9 %shard_map.39.ratio_ref = f32[8,128]{1,0:T(8,128)} custom-call(f32[16,128]{1,0:T(8,128)} %get-tuple-element.13.squares_ref), custom_call_target="tpu_custom_call" | custom-call | tf_op jit(solution)/shard_map/pallas_call | solution.py:440
  92.5 0.0 copy-start
  92.6 0.7 copy-done
  93.2 9.1 %shard_map.40 = f32[2048,1024]{1,0:T(8,128)} custom-call(f32[8,128]{1,0:T(8,128)S(1)} %copy-done, f32[2048,1024]{1,0:T(8,128)} %get-tuple-element.14.update_ref), custom_call_target="tpu_custom_call" | custom-call | tf_op jit(solution)/shard_map/pallas_call | solution.py:457
Async XLA Ops:
  92.5 0.7 copy-start

commit v3 on v2

--- a/solution.py
+++ b/solution.py
@@ -122,10 +122,9 @@
 
 def gather_kernel(
     og_ref, act_ref, update_ref, left_ref, stats_ref,
-    og_all, act_all, update_all, left_all,
+    og_all, act_all,
     og_own, og_cs, og_cr, og_xs, og_xr, og_zs, og_zr,
     act_own, act_cs, act_cr, act_xs, act_xr, act_ys, act_yr, act_fs, act_fr,
-    update_sem, left_sem,
 ):
     shard = og_ref.shape[0]
     half = shard // 2
@@ -223,26 +222,34 @@
         y_act(j).wait_recv()
         f_act(j, 1).start()
 
+    def send_local(a, j):
+        if j < features:
+            core_act(j).start()
+            own_act(j).start()
+        if a < chunks:
+            core_og(a).start()
+            own_og(a).start()
+
+    x_og(0, 0).start()
+    send_local(0, 0)
+    x_og(0, 0).wait_send()
+    x_og(0, 1).start()
+    x_og_arrived(0, 0)
+    z_og(0, 0).start()
+    x_og(0, 1).wait_send()
     x_act(0).start()
-    send_x(0)
-    for j in range(1, features):
-        x_act(j).start()
-    if chunks > 1:
-        send_x(1)
+    x_og_arrived(0, 1)
+    z_og(0, 1).start()
     for j in range(features):
-        core_act(j).start()
-        own_act(j).start()
-    for a in range(chunks):
-        core_og(a).start()
-        own_og(a).start()
-    pass_on_act(0)
-    pass_on_og(0)
-    if chunks > 2:
-        send_x(2)
-    pass_on_act_again(0)
-    for j in range(1, features):
+        x_act(j).wait_send()
+        if j + 1 < features:
+            x_act(j + 1).start()
+        elif chunks > 1:
+            send_x(1)
         pass_on_act(j)
-    for j in range(1, features):
+        if j == 0:
+            for n in range(1, max(chunks, features)):
+                send_local(n, n)
         pass_on_act_again(j)
     for j in range(features):
         own_act(j).wait()
@@ -250,16 +257,16 @@
         f_act(j, 0).wait_recv()
         f_act(j, 1).wait_recv()
 
-    def outgoing(s):
-        a, j = lax.div(s, features), lax.rem(s, features)
-        place = update_ref.at[span(a * BLK, BLK), span(j * BLK, BLK)]
-        return (
-            pltpu.make_async_copy(update_all.at[s], place, update_sem.at[s]),
-            pltpu.make_async_copy(left_all.at[s], left_ref.at[s], left_sem.at[s]),
-        )
-
     def step(s, carry):
         a, j = lax.div(s, features), lax.rem(s, features)
+
+        @pl.when((j == 0) & (a > 0) & (a + 1 < chunks))
+        def _():
+            pass_on_og(a + 1)
+
+        @pl.when((j == 0) & (a > 0) & (a + 2 < chunks))
+        def _():
+            send_x(a + 2)
 
         @pl.when(j == 0)
         def _():
@@ -270,22 +277,20 @@
 
         g = dot(og_all[a], act_all[j], TN)
         left, scaling, trace, update = first_iteration(g)
-        update_all[s] = update
-        left_all[s] = left
-        for copy in outgoing(s):
-            copy.start()
+        update_ref[s] = update
+        left_ref[s] = left
         stats_ref[s, 0:1, :] = jnp.broadcast_to(trace, (1, 128))
         stats_ref[s, 1:2, :] = jnp.broadcast_to(total(update * update), (1, 128))
         stats_ref[s, 2:3, :] = jnp.broadcast_to(scaling, (1, 128))
         stats_ref[s, 3:8, :] = jnp.zeros((5, 128), jnp.float32)
 
-        @pl.when((j == 0) & (a + 1 < chunks))
-        def _():
-            pass_on_og(a + 1)
-
-        @pl.when((j == 0) & (a + 3 < chunks))
-        def _():
-            send_x(a + 3)
+        @pl.when((s == 0) & (chunks > 1))
+        def _():
+            pass_on_og(1)
+
+        @pl.when((s == 0) & (chunks > 2))
+        def _():
+            send_x(2)
 
         return carry
 
@@ -294,17 +299,14 @@
     for a in range(chunks):
         core_og(a).wait_send()
         for k in range(2):
-            x_og(a, k).wait_send()
+            if a > 0:
+                x_og(a, k).wait_send()
             z_og(a, k).wait_send()
     for j in range(features):
         core_act(j).wait_send()
-        x_act(j).wait_send()
         y_act(j).wait_send()
         f_act(j, 0).wait_send()
         f_act(j, 1).wait_send()
-    for s in range(chunks * features):
-        for copy in outgoing(s):
-            copy.wait()
 
 
 def gathered_updates(og, act):
@@ -320,29 +322,25 @@
     return pl.pallas_call(
         gather_kernel,
         in_specs=[anywhere, anywhere],
-        out_specs=[anywhere, anywhere, pl.BlockSpec(memory_space=pltpu.VMEM)],
+        out_specs=[pl.BlockSpec(memory_space=pltpu.VMEM)] * 3,
         out_shape=[
-            jax.ShapeDtypeStruct((rows, width), jnp.float32),
-            jax.ShapeDtypeStruct((blocks, BLK, BLK), jnp.float32),
-            jax.ShapeDtypeStruct((blocks, 8, 128), jnp.float32),
+            pltpu.VMEM((blocks, BLK, BLK), jnp.float32),
+            pltpu.VMEM((blocks, BLK, BLK), jnp.float32),
+            pltpu.VMEM((blocks, 8, 128), jnp.float32),
         ],
         scratch_shapes=[
             pltpu.VMEM((chunks, tokens, BLK), jnp.bfloat16),
             pltpu.VMEM((features, tokens, BLK), jnp.bfloat16),
-            pltpu.VMEM((blocks, BLK, BLK), jnp.float32),
-            pltpu.VMEM((blocks, BLK, BLK), jnp.float32),
             one, one, one, two, two, two, two,
             act_one, act_one, act_one, act_one, act_one, act_one, act_one, act_two, act_two,
-            pltpu.SemaphoreType.DMA((blocks,)),
-            pltpu.SemaphoreType.DMA((blocks,)),
         ],
         compiler_params=pltpu.CompilerParams(
-            collective_id=0, has_side_effects=True, vmem_limit_bytes=56 * 2**20
+            collective_id=0, has_side_effects=True, vmem_limit_bytes=36 * 2**20
         ),
     )(og, act)
 
 
-def finish_kernel(counts_ref, stats_ref, left_ref, update_in, update_ref, squares_ref, coupled_ref, block_ref, sem):
+def finish_kernel(counts_ref, stats_ref, left_ref, update_in, update_ref, squares_ref, coupled_ref):
     del update_in
     features = counts_ref.shape[1]
     squares_ref[...] = jnp.zeros_like(squares_ref)
@@ -358,22 +356,10 @@
 
         @pl.when(count > 1)
         def _():
-            place = update_ref.at[
-                pl.ds(pl.multiple_of(a * BLK, BLK), BLK), pl.ds(pl.multiple_of(j * BLK, BLK), BLK)
-            ]
-            left_in = pltpu.make_async_copy(left_ref.at[s], coupled_ref, sem.at[0])
-            block_in = pltpu.make_async_copy(place, block_ref, sem.at[1])
-            left_in.start()
-            block_in.start()
-            left_in.wait()
-            block_in.wait()
-            coupled_ref[...] = stats_ref[s, 2:3, 0:1] * (coupled_ref[...] + SHIFT * identity())
-            later_iterations(count, coupled_ref, block_ref)
-            block_out = pltpu.make_async_copy(block_ref, place, sem.at[2])
-            block_out.start()
-            u = block_ref[...]
+            coupled_ref[...] = stats_ref[s, 2:3, 0:1] * (left_ref[s] + SHIFT * identity())
+            later_iterations(count, coupled_ref, update_ref.at[s])
+            u = update_ref[s]
             squares_ref[8:16, :] += jnp.broadcast_to(total(u * u), (8, 128))
-            block_out.wait()
 
         return carry
 
@@ -381,23 +367,18 @@
 
 
 def finished_updates(counts, stats, left, updates):
-    anywhere = pl.BlockSpec(memory_space=pl.ANY)
     vmem = pl.BlockSpec(memory_space=pltpu.VMEM)
     return pl.pallas_call(
         finish_kernel,
-        in_specs=[pl.BlockSpec(memory_space=pltpu.SMEM), vmem, anywhere, anywhere],
-        out_specs=[anywhere, vmem],
+        in_specs=[pl.BlockSpec(memory_space=pltpu.SMEM), vmem, vmem, vmem],
+        out_specs=[vmem, vmem],
         out_shape=[
-            jax.ShapeDtypeStruct(updates.shape, jnp.float32),
-            jax.ShapeDtypeStruct((16, 128), jnp.float32),
-        ],
-        scratch_shapes=[
-            pltpu.VMEM((BLK, BLK), jnp.float32),
-            pltpu.VMEM((BLK, BLK), jnp.float32),
-            pltpu.SemaphoreType.DMA((3,)),
-        ],
+            pltpu.VMEM(updates.shape, jnp.float32),
+            pltpu.VMEM((16, 128), jnp.float32),
+        ],
+        scratch_shapes=[pltpu.VMEM((BLK, BLK), jnp.float32)],
         input_output_aliases={3: 0},
-        compiler_params=pltpu.CompilerParams(vmem_limit_bytes=56 * 2**20),
+        compiler_params=pltpu.CompilerParams(vmem_limit_bytes=36 * 2**20),
     )(counts, stats, left, updates)
 
 
@@ -464,6 +445,44 @@
     )(ratio, updates)
 
 
+def scale_blocks_kernel(ratio_ref, update_ref, out_ref, scaled, sem):
+    features = out_ref.shape[1] // BLK
+
+    def place(s):
+        a, j = lax.div(s, features), lax.rem(s, features)
+        there = out_ref.at[
+            pl.ds(pl.multiple_of(a * BLK, BLK), BLK), pl.ds(pl.multiple_of(j * BLK, BLK), BLK)
+        ]
+        return pltpu.make_async_copy(scaled.at[s], there, sem.at[s])
+
+    def scale(s, carry):
+        scaled[s] = update_ref[s] * ratio_ref[0:1, 0:1]
+        place(s).start()
+        return carry
+
+    def wait(s, carry):
+        place(s).wait()
+        return carry
+
+    lax.fori_loop(0, scaled.shape[0], scale, 0)
+    lax.fori_loop(0, scaled.shape[0], wait, 0)
+
+
+def scaled_blocks(ratio, updates, shape):
+    vmem = pl.BlockSpec(memory_space=pltpu.VMEM)
+    return pl.pallas_call(
+        scale_blocks_kernel,
+        in_specs=[vmem, vmem],
+        out_specs=pl.BlockSpec(memory_space=pl.ANY),
+        out_shape=jax.ShapeDtypeStruct(shape, jnp.float32),
+        scratch_shapes=[
+            pltpu.VMEM(updates.shape, jnp.float32),
+            pltpu.SemaphoreType.DMA((updates.shape[0],)),
+        ],
+        compiler_params=pltpu.CompilerParams(vmem_limit_bytes=36 * 2**20),
+    )(ratio, updates)
+
+
 def gathered_first(activations, output_grads, iter_counts):
     act = lax.all_gather(activations, "dp", axis=0, tiled=True)
     og = lax.all_to_all(output_grads, "dp", split_axis=1, concat_axis=0, tiled=True)
@@ -475,8 +494,9 @@
     if sizes[0] == 4 and sizes[1] % 2 == 0 and sizes[2] == 2:
         updates, left, stats = gathered_updates(output_grads, activations)
         updates, squares = finished_updates(iter_counts, stats, left, updates)
-    else:
-        updates, squares = gathered_first(activations, output_grads, iter_counts)
+        shape = (output_grads.shape[1] // sizes[0], activations.shape[1])
+        return scaled_blocks(graft_ratio(squares), updates, shape)
+    updates, squares = gathered_first(activations, output_grads, iter_counts)
     return scaled_updates(graft_ratio(squares), updates)
 
 

time: 102 us -> 96 us (0.941)
  Pallas kernels: 100 us -> 86.2 us
  local copies, waits for them, and re-layouts: 1.99 us -> 9.85 us
    pallas_call x2, Pallas kernels: 73.8 us -> 63.4 us  [the longest x1 59.9 us: gathered_updates(): pl.pallas_call(gather_kernel, in_specs=[anywhere, anywhere], out_specs=[p...]
    unnamed x3 -> x11, local copies, waits for them, and re-layouts: 1.99 us -> 9.85 us
    pallas_call x1, Pallas kernels: 24.9 us -> 22.1 us  [graft_ratio(): pl.pallas_call(functools.partial(ratio_kernel, axes), in_specs=[vmem], ou...]
where the time goes in v3:
time: 96 us; the launch traced here: 96.1 us
  Pallas kernels  86.2 us (90%)
  local copies, waits for them, and re-layouts  9.85 us (10%)
    pallas_call x1, Pallas kernels, gathered_updates(): pl.pallas_call(gather_kernel, in_specs=[anywhere, anywhere], out_specs=[p...  59.9 us
    pallas_call x1, Pallas kernels, graft_ratio(): pl.pallas_call(functools.partial(ratio_kernel, axes), in_specs=[vmem], ou...  22.1 us
    unnamed x11, local copies, waits for them, and re-layouts  9.85 us
    pallas_call x1, Pallas kernels, scaled_blocks(): pl.pallas_call(scale_blocks_kernel, in_specs=[vmem, vmem], out_specs=pl.B...  3.47 us

profile of v3, /device:TPU:0, one launch (start us, length us, event | category | flops | bytes accessed | tf_op | source)
XLA Modules:
  0.0 96.1 jit_solution(1656900886446728914)
XLA Ops:
  0.0 0.8 copy.5.counts_ref
  0.8 0.0 copy-start.2
  0.8 1.0 %copy-done.2 = bf16[256,1024]{1,0:T(8,128)(2,1)S(1)} copy-done((bf16[256,1024]{1,0:T(8,128)(2,1)S(1)}, bf16[256,1024]{1,0:T(8,128)(2,1)}, u32[]{:S(2)}) %copy-start.2) | copy-done | bytes 524312
  1.8 59.9 %shard_map.37 = (f32[8,512,512]{2,1,0:T(8,128)S(1)}, f32[8,512,512]{2,1,0:T(8,128)S(1)}, f32[8,8,128]{2,1,0:T(8,128)S(1)}) custom-call(bf16[256,8192]{1,0:T(8,128)(2,1)} %og_ref.1, bf16[256,1024]{1,0:T(8,128)(2,1)S(1)} %copy-done.2), custom_call_target="tpu_custom_call" | custom-call | tf_op jit(solution)/shard_map/pallas_call | solution.py:322
  61.7 0.7 shard_map.38
  62.5 0.0 copy-start
  62.5 3.4 %copy-done = f32[8,512,512]{2,1,0:T(8,128)} copy-done((f32[8,512,512]{2,1,0:T(8,128)}, f32[8,512,512]{2,1,0:T(8,128)S(1)}, u32[]{:S(2)}) %copy-start) | copy-done | bytes 8388632
  65.9 0.0 copy-start.4
  65.9 0.6 copy-done.4
  66.5 22.1 %shard_map.39.ratio_ref = f32[8,128]{1,0:T(8,128)} custom-call(f32[16,128]{1,0:T(8,128)} %copy-done.4), custom_call_target="tpu_custom_call" | custom-call | tf_op jit(solution)/shard_map/pallas_call | solution.py:421
  88.6 0.0 copy-start.1
  88.6 3.4 %copy-done.1 = f32[8,512,512]{2,1,0:T(8,128)S(1)} copy-done((f32[8,512,512]{2,1,0:T(8,128)S(1)}, f32[8,512,512]{2,1,0:T(8,128)}, u32[]{:S(2)}) %copy-start.1) | copy-done | bytes 8388632
  92.0 0.0 copy-start.3
  92.0 0.7 copy-done.3
  92.7 3.5 %shard_map.40 = f32[2048,1024]{1,0:T(8,128)} custom-call(f32[8,128]{1,0:T(8,128)S(1)} %copy-done.3, f32[8,512,512]{2,1,0:T(8,128)S(1)} %copy-done.1), custom_call_target="tpu_custom_call" | custom-call | tf_op jit(solution)/shard_map/pallas_call | solution.py:473
Async XLA Ops:
  0.8 1.0 %copy-start.2 = (bf16[256,1024]{1,0:T(8,128)(2,1)S(1)}, bf16[256,1024]{1,0:T(8,128)(2,1)}, u32[]{:S(2)}) copy-start(bf16[256,1024]{1,0:T(8,128)(2,1)} %act_ref.1) | copy-start | bytes 1572868
  62.5 3.4 %copy-start = (f32[8,512,512]{2,1,0:T(8,128)}, f32[8,512,512]{2,1,0:T(8,128)S(1)}, u32[]{:S(2)}) copy-start(f32[8,512,512]{2,1,0:T(8,128)S(1)} %get-tuple-element.14.update_ref) | copy-start | bytes 25165828
  65.9 0.6 copy-start.4
  88.6 3.4 %copy-start.1 = (f32[8,512,512]{2,1,0:T(8,128)S(1)}, f32[8,512,512]{2,1,0:T(8,128)}, u32[]{:S(2)}) copy-start(f32[8,512,512]{2,1,0:T(8,128)} %copy-done) | copy-start | bytes 25165828
  92.0 0.7 copy-start.3
